TPU v7x, 768 devices: a whole 4x8x12 slice. The times are simulated.
768 devices in a mesh: dp: 2 (over core), expert: 12 (over z), tensor: 32 (over y, x).
Axes of the slice: x: 4, y: 8, z: 12, core: 2. Of those that a mesh axis runs over, the one named last changes fastest.
Arguments:
- grad_out: bfloat16 [6144, 4096], P(('dp', 'expert'), 'tensor'), may hold values from -6 to 6
- gates: float32 [6144, 2], P(('dp', 'expert')), may hold values from 0.1 to 1
- routes: int32 [6144, 2], P(('dp', 'expert')), may hold values from 0 to 11, all different within a row; in each aligned block of 256 rows (0 to 255, 256 to 511, ...) at most 64 rows name the same one
- hidden: bfloat16 [2, 12, 768, 4096], P('dp', 'expert'), may hold values from -6 to 6
- w_down: bfloat16 [12, 4096, 4096], P('expert', None, 'tensor'), may hold values from -0.09375 to 0.09375
Outputs:
- hidden_grad: bfloat16 [2, 12, 4096, 768], P('dp', 'expert', 'tensor')
- weight_grad: bfloat16 [12, 4096, 4096], P('expert', 'dp', 'tensor')
Inputs may be any that keep to these rules, and one draw needn't show every extreme that they name: `routes`: each token names two different experts; within the tokens of one data group (aligned blocks of 256 tokens) no expert is named more than 64 times, a bound that some block reaches.
All inputs are finite; a program needn't handle non-finite values.
Results may differ from a plain program's by a relative error of at most 0.0059.
Values may be sent and summed in bfloat16 or wider, within the bound.
A program may use at most 64 MiB of HBM per device.

v0:
```python
import jax
import jax.numpy as jnp
from jax import lax
from jax.sharding import PartitionSpec as P


def per_device(grad_out, gates, routes, hidden, w_down):
    expert_count = lax.axis_size("expert")
    slot_count = hidden.shape[2]
    capacity = slot_count // expert_count
    features = grad_out.shape[1]
    chosen = routes.reshape(-1)
    row_count = chosen.shape[0]
    onehot = (chosen[:, None] == jnp.arange(expert_count, dtype=jnp.int32)[None, :]).astype(
        jnp.int32
    )
    before = jnp.cumsum(onehot, axis=0) - onehot
    position = jnp.sum(before * onehot, axis=1)
    slot = chosen * capacity + position
    source = (
        jnp.full((slot_count,), row_count, jnp.int32)
        .at[slot]
        .set(jnp.arange(row_count, dtype=jnp.int32))
    )
    scaled = (gates[:, :, None] * grad_out[:, None, :].astype(jnp.float32)).reshape(
        row_count, features
    )
    padded = jnp.concatenate(
        [scaled.astype(jnp.bfloat16), jnp.zeros((1, features), jnp.bfloat16)], axis=0
    )
    outgoing = jnp.take(padded, source, axis=0)
    arrived = lax.all_to_all(outgoing, "expert", split_axis=0, concat_axis=0, tiled=True)
    weight = w_down[0]
    saved = hidden[0, 0]
    grad_hidden = lax.psum_scatter(
        lax.dot_general(
            weight, arrived, (((1,), (1,)), ((), ())), preferred_element_type=jnp.float32
        ),
        "tensor",
        scatter_dimension=0,
        tiled=True,
    )
    hidden_out = grad_hidden.astype(jnp.bfloat16)[None, None]
    local = lax.dot_general(
        saved, arrived, (((0,), (0,)), ((), ())), preferred_element_type=jnp.float32
    )
    local = local.astype(jnp.bfloat16).astype(jnp.float32)
    summed = lax.psum_scatter(local.astype(jnp.bfloat16), "dp", scatter_dimension=0, tiled=True)
    weight_out = summed[None]
    return (hidden_out, weight_out)


def solution(mesh):
    placed = (
        P(("dp", "expert"), "tensor"),
        P(("dp", "expert"), None),
        P(("dp", "expert"), None),
        P("dp", "expert", None, None),
        P("expert", None, "tensor"),
    )
    return jax.shard_map(
        per_device,
        mesh=mesh,
        in_specs=placed,
        out_specs=(P("dp", "expert", "tensor", None), P("expert", "dp", "tensor")),
        check_vma=False,
    )
```

profile of v0, /device:TPU:16, one launch (start us, length us, event | category | flops | bytes accessed | tf_op | source)
XLA Modules:
  0.0 329.5 jit_solution(16342263509865902975)
XLA Ops:
  7.2 0.9 copy.10
  8.1 0.1 eq.29
  8.3 0.1 eq.25
  8.4 0.7 broadcast_multiply_fusion
  9.1 1.1 reduce-window.6
  10.3 0.2 slice_reduce_fusion
  10.6 0.1 copy.9
  10.8 0.1 mul.39
  11.0 2.4 scatter_custom_fusion
  13.5 0.8 copy.13
  14.3 0.1 mul.41
  14.4 0.1 broadcast_in_dim.29
  14.5 0.9 mul.43
  15.4 0.1 multiply_convert_fusion
  15.6 1.9 gather_fusion
  17.5 0.2 broadcast_select_fusion
  17.7 28.9 %all_to_all.9 = bf16[12,64,128]{2,1,0:T(8,128)(2,1)S(1)} all-to-all(bf16[12,64,128]{2,1,0:T(8,128)(2,1)S(1)} %broadcast_select_fusion), channel_id=1, replica_groups=mesh['dp'=2,'expert'=12,'tensor'=32] {'expert'}, dimensions={0} | all-to-all | bytes 393216 | tf_op jit(solution)/shard_map/all_to_all | solution.py:32
  46.6 4.8 %fusion.5 = bf16[4096,128]{0,1:T(8,128)(2,1)} fusion(bf16[768,128]{1,0:T(8,128)(2,1)S(1)} %bitcast.33, bf16[1,1,768,4096]{3,2,1,0:T(8,128)(2,1)} %param.8), kind=kOutput, calls=%fused_computation.6 | convolution fusion | flops 805830656 | bytes 7536640 | tf_op jit(solution)/shard_map/dot_general | solution.py:44
  51.5 6.4 %convolution_bitcast_fusion = f32[4096,768]{0,1:T(8,128)} fusion(bf16[768,128]{1,0:T(8,128)(2,1)S(1)} %bitcast.34, bf16[1,4096,128]{2,1,0:T(8,128)(2,1)S(1)} %copy-done), kind=kOutput, calls=%fused_computation.2 | convolution fusion | flops 805306368 | bytes 13828096 | tf_op jit(solution)/shard_map/dot_general | solution.py:36
  57.9 7.8 %reduce-scatter.5.cloned.1.call-done = bf16[2048,128]{0,1:T(8,128)(2,1)} async-done(((bf16[4096,128]{0,1:T(8,128)(2,1)}), bf16[2048,128]{0,1:T(8,128)(2,1)}) %reduce-scatter.5.cloned.1.call-update) | async-done | bytes 524304 | tf_op jit(solution)/shard_map/reduce_scatter | solution.py:48
  65.7 2.0 copy.15
  67.7 253.1 %reduce-scatter.3.cloned.1.call-done = f32[128,768]{0,1:T(8,128)} async-done(((f32[4096,768]{0,1:T(8,128)}), f32[128,768]{0,1:T(8,128)}) %reduce-scatter.3.cloned.1.call-update) | async-done | bytes 393232 | tf_op jit(solution)/shard_map/reduce_scatter | solution.py:35
  320.8 1.0 convert_bitcast_fusion
  321.8 0.8 copy.14
  (20 shorter events, 0.3 us)
Async XLA Ops:
  7.2 44.3 %copy-start = (bf16[1,4096,128]{2,1,0:T(8,128)(2,1)S(1)}, bf16[1,4096,128]{2,1,0:T(8,128)(2,1)}, u32[]{:S(2)}) copy-start(bf16[1,4096,128]{2,1,0:T(8,128)(2,1)} %param.9) | copy-start | bytes 3145732
  7.2 58.5 %reduce-scatter.5.cloned.1.call-start = ((), (), s32[]{:S(2)}) async-start(), calls=%async_computation.4 | async-start | bytes 1572864 | tf_op jit(solution)/shard_map/reduce_scatter | solution.py:48
  51.5 269.4 %reduce-scatter.3.cloned.1.call-start = ((), (), s32[]{:S(2)}) async-start(), calls=%async_computation.3 | async-start | bytes 12976128 | tf_op jit(solution)/shard_map/reduce_scatter | solution.py:35
Sparse Core Ops, SparseCore 0:
  51.6 14.0 reduce-scatter.4
  71.8 248.9 reduce-scatter.2
where the time goes:
time: 330 us; the launch traced here: 329 us
  waiting for transfers between devices  261 us (79%)
  blocking collectives  28.9 us (9%)
  between operations  14.2 us (4%)
  matrix products  11.2 us (3%)
  local copies, waits for them, and re-layouts  10.9 us (3%)
  other arithmetic  3.32 us (1%)
    reduce_scatter x1, waiting for transfers between devices, per_device(): lax.psum_scatter(lax.dot_general(weight, arrived, (((1,), (1,)), ((), ())...  253 us
    all_to_all x1, blocking collectives, per_device(): lax.all_to_all(outgoing, 'expert', split_axis=0, concat_axis=0, tiled=True)  28.9 us
    reduce_scatter x1, waiting for transfers between devices, per_device(): lax.psum_scatter(local.astype(jnp.bfloat16), 'dp', scatter_dimension=0, t...  7.78 us
  transfers between devices with their start and end apart: 2, of which 2 were waited for; matrix products, arithmetic and copies ran while one was open for 3% of the time, Pallas kernels for 0%

commit v1 on v0

v1 whole, which is shorter than its diff:
```python
import functools

import jax
import jax.numpy as jnp
from jax import lax
from jax.experimental import pallas as pl
from jax.experimental.pallas import tpu as pltpu
from jax.sharding import PartitionSpec as P

MESH = pl.DeviceIdType.MESH
RING_X = 4
CHUNKS = 4
PIECES = 8


def kernel(
    ring_e,
    ring_x,
    ring_y,
    grad_ref,
    gates_ref,
    routes_ref,
    hidden_ref,
    w_ref,
    hg_ref,
    wg_ref,
    saved,
    weight,
    arrived,
    outgoing,
    place,
    gate_of,
    flipped,
    prod,
    part_out,
    part_in,
    local,
    other,
    saved_sem,
    own_sem,
    z_send,
    z_recv,
    w_send,
    w_recv,
    f_send,
    f_recv,
    x_send,
    x_recv,
    r_send,
    r_recv,
    y_send,
    y_recv,
    g_send,
    g_recv,
):
    tokens = grad_ref.shape[0]
    cap = arrived.shape[2]
    features = arrived.shape[3]
    group = ring_e // CHUNKS
    rows = group * cap
    half_y = ring_y // 2
    units = prod.shape[3]
    half_units = other.shape[0]

    core = lax.axis_index("dp")
    me = lax.axis_index("expert")
    flat = lax.axis_index("tensor")
    y, x = flat // ring_x, lax.rem(flat, ring_x)
    sibling = {"dp": 1 - core}

    def at_x(step):
        return {"tensor": y * ring_x + lax.rem(x + step + ring_x, ring_x)}

    def at_y(step):
        return {"tensor": lax.rem(y + step + ring_y, ring_y) * ring_x + x}

    def peer(number):
        offset = (number + 1) // 2 if number % 2 else -(number // 2)
        return lax.rem(me + offset + ring_e, ring_e)

    def mirror(number):
        if number == ring_e - 1:
            return number
        return number + 1 if number % 2 else number - 1

    def send(src, dst, send_sem, recv_sem, where):
        return pltpu.make_async_remote_copy(
            src_ref=src,
            dst_ref=dst,
            send_sem=send_sem,
            recv_sem=recv_sem,
            device_id=where,
            device_id_type=MESH,
        )

    barrier = pltpu.get_barrier_semaphore()
    for number in range(1, ring_e):
        pl.semaphore_signal(
            barrier, inc=1, device_id={"expert": peer(number)}, device_id_type=MESH
        )
    for step in (1, -1, 2):
        pl.semaphore_signal(barrier, inc=1, device_id=at_x(step), device_id_type=MESH)
    for step in (1, -1):
        pl.semaphore_signal(barrier, inc=1, device_id=at_y(step), device_id_type=MESH)
    pl.semaphore_signal(barrier, inc=1, device_id=sibling, device_id_type=MESH)

    own = pltpu.make_async_copy(w_ref.at[:, x], weight.at[0], own_sem)
    own.start()
    saved_copies = []
    for number in range(ring_e):
        copy = pltpu.make_async_copy(
            hidden_ref.at[peer(number)],
            saved.at[pl.ds(number * cap, cap)],
            saved_sem.at[number],
        )
        copy.start()
        saved_copies.append(copy)

    sublanes = place.shape[0]
    expert_ids = lax.broadcasted_iota(jnp.int32, (sublanes, tokens), 0)
    first = routes_ref[0:1, :] == expert_ids
    second = routes_ref[1:2, :] == expert_ids
    member = jnp.where(first | second, 1.0, 0.0).astype(jnp.bfloat16)
    earlier = jnp.where(
        lax.broadcasted_iota(jnp.int32, (tokens, tokens), 0)
        < lax.broadcasted_iota(jnp.int32, (tokens, tokens), 1),
        1.0,
        0.0,
    ).astype(jnp.bfloat16)
    before = jnp.dot(member, earlier, preferred_element_type=jnp.float32)
    place[...] = jnp.where(first | second, before.astype(jnp.int32), -1)
    gate_of[...] = jnp.where(first, gates_ref[0:1, :], 0.0) + jnp.where(
        second, gates_ref[1:2, :], 0.0
    )

    pl.semaphore_wait(barrier, ring_e - 1 + 3 + 2 + 1)

    half_rows = pl.ds(core * half_y, half_y)
    w_copies = {}
    for step, slot in ((1, 1), (-1, 3), (2, 2)):
        copy = send(
            w_ref.at[half_rows, lax.rem(x + step + ring_x, ring_x)],
            weight.at[slot, half_rows],
            w_send.at[slot],
            w_recv.at[slot],
            at_x(step),
        )
        copy.start()
        w_copies[slot] = copy

    z_copies = {}
    slot_ids = lax.broadcasted_iota(jnp.int32, (cap, tokens), 0)
    for chunk in range(CHUNKS):
        masks, scales = [], []
        numbers = range(chunk * group, (chunk + 1) * group)
        for number in numbers:
            expert = peer(number)
            hit = slot_ids == place[pl.ds(expert, 1), :]
            masks.append(jnp.where(hit, 1.0, 0.0).astype(jnp.bfloat16))
            scales.append(
                jnp.sum(
                    jnp.where(hit, gate_of[pl.ds(expert, 1), :], 0.0), axis=1, keepdims=True
                )
            )
        picked = jnp.dot(
            jnp.concatenate(masks, axis=0), grad_ref[...], preferred_element_type=jnp.float32
        )
        scaled = (jnp.concatenate(scales, axis=0) * picked).astype(jnp.bfloat16)
        for index, number in enumerate(numbers):
            block = scaled[index * cap : (index + 1) * cap]
            if number == 0:
                arrived[0, 0] = block
                continue
            outgoing[number] = block
            copy = send(
                outgoing.at[number],
                arrived.at[0, mirror(number)],
                z_send.at[number],
                z_recv.at[mirror(number)],
                {"expert": peer(number)},
            )
            copy.start()
            z_copies[number] = copy

    x_copies, r_copies, f_copies, y_copies = {}, {}, {}, {}

    def gather(chunk):
        blocks = pl.ds(chunk * group, group)
        for number in range(chunk * group, (chunk + 1) * group):
            if number > 0:
                z_copies[mirror(number)].wait_recv()
        for step, slot, lane in ((1, 1, 0), (-1, 3, 1)):
            copy = send(
                arrived.at[0, blocks],
                arrived.at[slot, blocks],
                x_send.at[chunk, lane],
                x_recv.at[chunk, lane],
                at_x(step),
            )
            copy.start()
            x_copies[chunk, lane] = copy

    def relay(chunk):
        blocks = pl.ds(chunk * group, group)
        lane = chunk % 2
        x_copies[chunk, lane].wait_recv()
        copy = send(
            arrived.at[(1, 3)[lane], blocks],
            arrived.at[2, blocks],
            r_send.at[chunk],
            r_recv.at[chunk],
            at_x((1, -1)[lane]),
        )
        copy.start()
        r_copies[chunk] = copy

    def share_weight():
        own.wait()
        for slot in (1, 3, 2):
            w_copies[slot].wait_recv()
            copy = send(
                weight.at[slot, half_rows],
                weight.at[slot, half_rows],
                f_send.at[slot],
                f_recv.at[slot],
                sibling,
            )
            copy.start()
            f_copies[slot] = copy
        for slot in (1, 3, 2):
            f_copies[slot].wait_recv()

    def product(chunk):
        x_copies[chunk, 1 - chunk % 2].wait_recv()
        r_copies[chunk].wait_recv()
        blocks = pl.ds(chunk * group, group)
        left = jnp.concatenate(
            [arrived[slot, blocks].reshape(rows, features) for slot in range(ring_x)], axis=1
        )
        for pair in range(half_y):
            right = []
            for number in (2 * pair, 2 * pair + 1):
                target = lax.rem(y + number - (half_y - 1) + ring_y, ring_y)
                right.append(
                    jnp.concatenate([weight[slot, target] for slot in range(ring_x)], axis=1)
                )
            both = lax.dot_general(
                left,
                jnp.concatenate(right, axis=0),
                (((1,), (1,)), ((), ())),
                preferred_element_type=jnp.float32,
            )
            prod[chunk, 2 * pair] = both[:, :units]
            prod[chunk, 2 * pair + 1] = both[:, units:]

    def first_step(chunk, lane):
        return 0 if chunk % 2 == lane else 1

    def reduce_step(chunk, lane, step):
        distance = half_y - step if lane == 0 else step - half_y
        number = distance + half_y - 1
        if number < 0:
            number += ring_y
        total = prod[chunk, number]
        if step > first_step(chunk, lane):
            y_copies[lane, chunk, step - 1].wait_recv()
            total = total + part_in[lane, chunk, step - 1].astype(jnp.float32)
        part_out[lane, chunk, step] = total.astype(jnp.bfloat16)
        copy = send(
            part_out.at[lane, chunk, step],
            part_in.at[lane, chunk, step],
            y_send.at[lane, chunk, step],
            y_recv.at[lane, chunk, step],
            at_y((1, -1)[lane]),
        )
        copy.start()
        y_copies[lane, chunk, step] = copy

    def start_reduce(chunk):
        for lane in (chunk % 2, 1 - chunk % 2):
            reduce_step(chunk, lane, first_step(chunk, lane))

    def finish(chunk):
        last = half_y - 1
        y_copies[0, chunk, last].wait_recv()
        y_copies[1, chunk, last].wait_recv()
        total = (
            prod[chunk, half_y - 1]
            + part_in[0, chunk, last].astype(jnp.float32)
            + part_in[1, chunk, last].astype(jnp.float32)
        ).astype(jnp.bfloat16)
        for index in range(group):
            source = peer(chunk * group + index)
            hg_ref[pl.ds(pl.multiple_of(source * cap, cap), cap), :] = total[
                index * cap : (index + 1) * cap
            ]

    piece_units = local.shape[0] // PIECES

    def weight_piece(piece):
        if piece == 0:
            for copy in saved_copies:
                copy.wait()
            flipped[...] = arrived[0].reshape(ring_e * cap, features).T
        base = (1 - core) * half_units if piece < PIECES // 2 else core * half_units
        start = base + (piece % (PIECES // 2)) * piece_units
        start = pl.multiple_of(start, piece_units)
        block = jnp.dot(
            flipped[...],
            saved[:, pl.ds(start, piece_units)],
            preferred_element_type=jnp.float32,
        )
        local[pl.ds(start, piece_units), :] = block.T.astype(jnp.bfloat16)

    theirs = pl.ds(pl.multiple_of((1 - core) * half_units, half_units), half_units)
    ours = pl.ds(pl.multiple_of(core * half_units, half_units), half_units)
    swap = send(local.at[theirs], other, g_send, g_recv, sibling)

    def advance(pieces):
        piece = next(pieces, None)
        if piece is not None:
            weight_piece(piece)
            if piece == PIECES // 2 - 1:
                swap.start()

    gather(0)
    gather(1)
    relay(0)
    gather(2)
    relay(1)
    share_weight()
    product(0)
    start_reduce(0)
    gather(3)
    relay(2)
    product(1)
    start_reduce(1)
    relay(3)
    product(2)
    start_reduce(2)
    product(3)
    start_reduce(3)

    pieces = iter(range(PIECES))
    for step in range(1, half_y):
        for chunk in range(CHUNKS):
            for lane in (0, 1):
                if step > first_step(chunk, lane):
                    reduce_step(chunk, lane, step)
            advance(pieces)
    for _ in range(PIECES):
        advance(pieces)
    for chunk in range(CHUNKS):
        finish(chunk)

    swap.wait_recv()
    wg_ref[...] = (local[ours].astype(jnp.float32) + other[...].astype(jnp.float32)).astype(
        jnp.bfloat16
    )

    for copies in (w_copies, z_copies, x_copies, r_copies, f_copies, y_copies):
        for copy in copies.values():
            copy.wait_send()
    swap.wait_send()


def per_device(grad_out, gates, routes, hidden, w_down):
    ring_e = lax.axis_size("expert")
    ring_t = lax.axis_size("tensor")
    ring_x = RING_X
    ring_y = ring_t // ring_x
    tokens, features = grad_out.shape
    slots, units = hidden.shape[2], hidden.shape[3]
    cap = slots // ring_e
    own_units = units // ring_t
    rows = slots // CHUNKS
    half_y = ring_y // 2
    sublanes = -(-ring_e // 16) * 16
    bf16, f32 = jnp.bfloat16, jnp.float32
    dma = pltpu.SemaphoreType.DMA
    vmem = pl.BlockSpec(memory_space=pltpu.VMEM)
    hbm = pl.BlockSpec(memory_space=pl.ANY)
    hidden_grad, weight_grad = pl.pallas_call(
        functools.partial(kernel, ring_e, ring_x, ring_y),
        out_shape=(
            jax.ShapeDtypeStruct((slots, own_units), bf16),
            jax.ShapeDtypeStruct((units // 2, features), bf16),
        ),
        in_specs=[vmem, vmem, vmem, hbm, hbm],
        out_specs=(vmem, vmem),
        scratch_shapes=[
            pltpu.VMEM((slots, units), bf16),
            pltpu.VMEM((ring_x, ring_y, own_units, features), bf16),
            pltpu.VMEM((ring_x, ring_e, cap, features), bf16),
            pltpu.VMEM((ring_e, cap, features), bf16),
            pltpu.VMEM((sublanes, tokens), jnp.int32),
            pltpu.VMEM((sublanes, tokens), f32),
            pltpu.VMEM((features, slots), bf16),
            pltpu.VMEM((CHUNKS, ring_y, rows, own_units), f32),
            pltpu.VMEM((2, CHUNKS, half_y, rows, own_units), bf16),
            pltpu.VMEM((2, CHUNKS, half_y, rows, own_units), bf16),
            pltpu.VMEM((units, features), bf16),
            pltpu.VMEM((units // 2, features), bf16),
            dma((ring_e,)),
            dma,
            dma((ring_e,)),
            dma((ring_e,)),
            dma((ring_x,)),
            dma((ring_x,)),
            dma((ring_x,)),
            dma((ring_x,)),
            dma((CHUNKS, 2)),
            dma((CHUNKS, 2)),
            dma((CHUNKS,)),
            dma((CHUNKS,)),
            dma((2, CHUNKS, half_y)),
            dma((2, CHUNKS, half_y)),
            dma,
            dma,
        ],
        compiler_params=pltpu.CompilerParams(
            collective_id=0, has_side_effects=True, vmem_limit_bytes=40 * 1024 * 1024
        ),
        cost_estimate=pl.CostEstimate(
            flops=4 * units * slots * features,
            bytes_accessed=2 * units * (slots + 2 * features),
            transcendentals=0,
        ),
    )(
        grad_out,
        gates.T,
        routes.T,
        hidden.reshape(ring_e, cap, units),
        w_down.reshape(ring_y, ring_x, own_units, features),
    )
    return hidden_grad.T[None, None], weight_grad[None]


def solution(mesh):
    placed = (
        P(("dp", "expert"), "tensor"),
        P(("dp", "expert"), None),
        P(("dp", "expert"), None),
        P("dp", "expert", None, None),
        P("expert", None, "tensor"),
    )
    return jax.shard_map(
        per_device,
        mesh=mesh,
        in_specs=placed,
        out_specs=(P("dp", "expert", "tensor", None), P("expert", "dp", "tensor")),
        check_vma=False,
    )
```

time: 330 us -> 62.6 us (0.19)
  the two profiles are of different devices: /device:TPU:16 before, /device:TPU:4 now
where the time goes in v1:
time: 62.6 us; the launch traced here: 62.3 us
  Pallas kernels  53.8 us (86%)
  local copies, waits for them, and re-layouts  7.82 us (12%)
  between operations  0.65 us (1%)
    pallas_call x1, Pallas kernels, per_device(): pl.pallas_call(functools.partial(kernel, ring_e, ring_x, ring_y), out_sha...  53.8 us
    unnamed x12, local copies, waits for them, and re-layouts  7.82 us

profile of v1, /device:TPU:4, one launch (start us, length us, event | category | flops | bytes accessed | tf_op | source)
XLA Modules:
  0.0 62.3 jit_solution(599171607178377441)
XLA Ops:
  0.6 0.0 copy-start
  0.6 2.8 %copy-done = bf16[1,1,768,4096]{3,2,1,0:T(8,128)(2,1)S(1)} copy-done((bf16[1,1,768,4096]{3,2,1,0:T(8,128)(2,1)S(1)}, bf16[1,1,768,4096]{3,2,1,0:T(8,128)(2,1)}, u32[]{:S(2)}) %copy-start) | copy-done | bytes 6291480
  3.4 0.0 copy-start.1
  3.4 1.2 %copy-done.1 = bf16[1,4096,128]{2,1,0:T(8,128)(2,1)S(1)} copy-done((bf16[1,4096,128]{2,1,0:T(8,128)(2,1)S(1)}, bf16[1,4096,128]{2,1,0:T(8,128)(2,1)}, u32[]{:S(2)}) %copy-start.1) | copy-done | bytes 1048600
  4.6 0.0 copy-start.2
  4.6 0.8 %copy-done.2 = bf16[256,128]{1,0:T(8,128)(2,1)S(1)} copy-done((bf16[256,128]{1,0:T(8,128)(2,1)S(1)}, bf16[256,128]{1,0:T(8,128)(2,1)}, u32[]{:S(2)}) %copy-start.2) | copy-done | bytes 65560
  5.5 0.0 copy-start.3
  5.5 0.7 %copy-done.3 = f32[256,2]{0,1:T(2,128)S(1)} copy-done((f32[256,2]{0,1:T(2,128)S(1)}, f32[256,2]{0,1:T(2,128)}, u32[]{:S(2)}) %copy-start.3) | copy-done | bytes 2072
  6.2 0.0 copy-start.4
  6.2 0.7 %copy-done.4 = s32[256,2]{0,1:T(2,128)S(1)} copy-done((s32[256,2]{0,1:T(2,128)S(1)}, s32[256,2]{0,1:T(2,128)}, u32[]{:S(2)}) %copy-start.4) | copy-done | bytes 2072
  6.8 53.8 %shard_map.68 = (bf16[768,128]{1,0:T(8,128)(2,1)S(1)}, bf16[2048,128]{1,0:T(8,128)(2,1)S(1)}) custom-call(bf16[256,128]{1,0:T(8,128)(2,1)S(1)} %copy-done.2, f32[2,256]{1,0:T(2,128)S(1)} %bitcast.12, s32[2,256]{1,0:T(2,128)S(1)} %bitcast.13, bf16[12,64,4096]{2,1,0:T(8,128)(2,1)S(1)} %bitcast.8, bf16[8,4,128,128]{3,2,1,0:T(8,128)(2,1)S(1)} %bitcast.9), custom_call_target="tpu_custom_call" | custom-call | flops 1610612736 | bytes 8388608 | tf_op jit(solution)/shard_map/pallas_call | solution.py:383
  60.7 0.8 %copy.7 = bf16[1,1,128,768]{3,2,1,0:T(8,128)(2,1)} copy(bf16[1,1,128,768]{2,3,1,0:T(8,128)(2,1)S(1)} %bitcast.11) | data formatting | bytes 393216
  61.5 0.8 %copy.9 = bf16[1,2048,128]{2,1,0:T(8,128)(2,1)} copy(bf16[1,2048,128]{2,1,0:T(8,128)(2,1)S(1)} %bitcast.10) | data formatting | bytes 1048576
Async XLA Ops:
  0.6 2.8 %copy-start = (bf16[1,1,768,4096]{3,2,1,0:T(8,128)(2,1)S(1)}, bf16[1,1,768,4096]{3,2,1,0:T(8,128)(2,1)}, u32[]{:S(2)}) copy-start(bf16[1,1,768,4096]{3,2,1,0:T(8,128)(2,1)} %param.8) | copy-start | bytes 18874372
  3.4 1.2 %copy-start.1 = (bf16[1,4096,128]{2,1,0:T(8,128)(2,1)S(1)}, bf16[1,4096,128]{2,1,0:T(8,128)(2,1)}, u32[]{:S(2)}) copy-start(bf16[1,4096,128]{2,1,0:T(8,128)(2,1)} %param.9) | copy-start | bytes 3145732
  4.6 0.8 %copy-start.2 = (bf16[256,128]{1,0:T(8,128)(2,1)S(1)}, bf16[256,128]{1,0:T(8,128)(2,1)}, u32[]{:S(2)}) copy-start(bf16[256,128]{1,0:T(8,128)(2,1)} %grad_ref.1) | copy-start | bytes 196612
  5.5 0.7 %copy-start.3 = (f32[256,2]{0,1:T(2,128)S(1)}, f32[256,2]{0,1:T(2,128)}, u32[]{:S(2)}) copy-start(f32[256,2]{0,1:T(2,128)} %param.6) | copy-start | bytes 6148
  6.2 0.7 %copy-start.4 = (s32[256,2]{0,1:T(2,128)S(1)}, s32[256,2]{0,1:T(2,128)}, u32[]{:S(2)}) copy-start(s32[256,2]{0,1:T(2,128)} %param.7) | copy-start | bytes 6148

commit v2 on v1

v2 whole, which is shorter than its diff:
```python
import functools

import jax
import jax.numpy as jnp
from jax import lax
from jax.experimental import pallas as pl
from jax.experimental.pallas import tpu as pltpu
from jax.sharding import PartitionSpec as P

MESH = pl.DeviceIdType.MESH
RING_X = 4
CHUNKS = 4
PIECES = 8
BOUNDS = [0, 3, 5, 8]
SCHEDULE = tuple(
    step
    for steps in (
        ("W0", "W1", "W2", "g0", "g1", "g2", "g3", "s0", "s1"),
        ("s2", "a", "a", "p00", "S0", "p10", "S1", "p20", "S2"),
        ("p30", "S3", "a", "L0", "a", "L1", "a", "L2", "a"),
        ("L3", "p01", "B02", "a", "p11", "B12", "a", "p21", "B22"),
        ("p31", "B32", "p02", "B03", "p12", "B13", "p22", "B23", "p32"),
        ("B33",),
    )
    for step in steps
)


def kernel(
    ring_e,
    ring_x,
    ring_y,
    grad_hbm,
    gates_hbm,
    routes_hbm,
    hidden_ref,
    w_ref,
    hg_hbm,
    wg_hbm,
    grad_ref,
    gates_ref,
    routes_ref,
    saved,
    staged,
    weight,
    arrived,
    outgoing,
    place,
    gate_of,
    flipped,
    prod,
    part_out,
    part_in,
    local,
    other,
    gathered_grad,
    hg_ref,
    wg_ref,
    small_sem,
    saved_sem,
    staged_sem,
    z_send,
    z_recv,
    w_send,
    w_recv,
    f_send,
    f_recv,
    x_send,
    x_recv,
    y_send,
    y_recv,
    g_send,
    g_recv,
    out_sem,
):
    tokens = grad_ref.shape[0]
    cap = arrived.shape[2]
    features = arrived.shape[3]
    group = ring_e // CHUNKS
    rows = group * cap
    half_y = ring_y // 2
    units = prod.shape[3]
    half_units = other.shape[0]

    core = lax.axis_index("dp")
    me = lax.axis_index("expert")
    flat = lax.axis_index("tensor")
    y, x = flat // ring_x, lax.rem(flat, ring_x)
    sibling = {"dp": 1 - core}

    def at_x(step):
        return {"tensor": y * ring_x + lax.rem(x + step + ring_x, ring_x)}

    def at_y(step):
        return {"tensor": lax.rem(y + step + ring_y, ring_y) * ring_x + x}

    offsets = [0, 1, -1, ring_e // 2]
    for offset in range(ring_e // 2 - 1, 1, -1):
        offsets += [offset, -offset]

    def peer(number):
        return lax.rem(me + offsets[number] + ring_e, ring_e)

    def mirror(number):
        if 2 * offsets[number] == ring_e:
            return number
        return offsets.index(-offsets[number])

    def send(src, dst, send_sem, recv_sem, where):
        return pltpu.make_async_remote_copy(
            src_ref=src,
            dst_ref=dst,
            send_sem=send_sem,
            recv_sem=recv_sem,
            device_id=where,
            device_id_type=MESH,
        )

    barrier = pltpu.get_barrier_semaphore()
    for number in range(1, ring_e):
        pl.semaphore_signal(
            barrier, inc=1, device_id={"expert": peer(number)}, device_id_type=MESH
        )
    for step in (1, -1, 2):
        pl.semaphore_signal(barrier, inc=1, device_id=at_x(step), device_id_type=MESH)
    for step in (1, -1):
        pl.semaphore_signal(barrier, inc=1, device_id=at_y(step), device_id_type=MESH)
    pl.semaphore_signal(barrier, inc=1, device_id=sibling, device_id_type=MESH)

    small = [
        pltpu.make_async_copy(src, dst, small_sem.at[index])
        for index, (src, dst) in enumerate(
            ((routes_hbm, routes_ref), (gates_hbm, gates_ref), (grad_hbm, grad_ref))
        )
    ]
    for copy in small:
        copy.start()

    distances = [4, 3, -3, 2, -2, 1, -1, 0]
    bounds = BOUNDS
    parts = [pl.ds(a, b - a) for a, b in zip(bounds, bounds[1:])]
    staged_copies = []
    for index, distance in enumerate(distances):
        copy = pltpu.make_async_copy(
            w_ref.at[lax.rem(y + distance + ring_y, ring_y)],
            staged.at[index],
            staged_sem.at[index],
        )
        copy.start()
        staged_copies.append(copy)
    small[0].wait()
    small[1].wait()

    sublanes = place.shape[0]
    expert_ids = lax.broadcasted_iota(jnp.int32, (sublanes, tokens), 0)
    first = routes_ref[0:1, :] == expert_ids
    second = routes_ref[1:2, :] == expert_ids
    member = jnp.where(first | second, 1.0, 0.0).astype(jnp.bfloat16)
    earlier = jnp.where(
        lax.broadcasted_iota(jnp.int32, (tokens, tokens), 0)
        < lax.broadcasted_iota(jnp.int32, (tokens, tokens), 1),
        1.0,
        0.0,
    ).astype(jnp.bfloat16)
    before = jnp.dot(member, earlier, preferred_element_type=jnp.float32)
    place[...] = jnp.where(first | second, before.astype(jnp.int32), -1)
    gate_of[...] = jnp.where(first, gates_ref[0:1, :], 0.0) + jnp.where(
        second, gates_ref[1:2, :], 0.0
    )

    small[2].wait()

    slot_ids = lax.broadcasted_iota(jnp.int32, (cap, tokens), 0)
    for chunk in range(CHUNKS):
        masks, scales = [], []
        numbers = range(chunk * group, (chunk + 1) * group)
        for number in numbers:
            expert = peer(number)
            hit = slot_ids == place[pl.ds(expert, 1), :]
            masks.append(jnp.where(hit, 1.0, 0.0).astype(jnp.bfloat16))
            scales.append(
                jnp.sum(
                    jnp.where(hit, gate_of[pl.ds(expert, 1), :], 0.0), axis=1, keepdims=True
                )
            )
        picked = jnp.dot(
            jnp.concatenate(masks, axis=0), grad_ref[...], preferred_element_type=jnp.float32
        )
        scaled = (jnp.concatenate(scales, axis=0) * picked).astype(jnp.bfloat16)
        for index, number in enumerate(numbers):
            block = scaled[index * cap : (index + 1) * cap]
            if number == 0:
                arrived[0, 0] = block
            else:
                outgoing[number] = block

    pl.semaphore_wait(barrier, ring_e - 1 + 3 + 2 + 1)

    z_copies = {}
    for number in range(1, ring_e):
        copy = send(
            outgoing.at[number],
            arrived.at[0, mirror(number)],
            z_send.at[number],
            z_recv.at[mirror(number)],
            {"expert": peer(number)},
        )
        copy.start()
        z_copies[number] = copy

    half_rows = pl.ds(pl.multiple_of(core * (units // 2), units // 2), units // 2)
    w_copies = {}
    for copy in staged_copies:
        copy.wait()

    def chip(step):
        return lax.rem(x + step + ring_x, ring_x)

    def send_weight(number):
        part = parts[number]
        for lane, step, slot in ((4, 2, 1), (0, 1, 0), (1, -1, 2)):
            copy = send(
                staged.at[part, chip(step), half_rows],
                weight.at[slot, part, half_rows],
                w_send.at[number, lane],
                w_recv.at[number, lane],
                at_x(step),
            )
            copy.start()
            w_copies[number, lane] = copy

    saved_copies = []
    for number in range(ring_e):
        copy = pltpu.make_async_copy(
            hidden_ref.at[peer(number)],
            saved.at[pl.ds(number * cap, cap)],
            saved_sem.at[number],
        )
        copy.start()
        saved_copies.append(copy)

    x_copies, f_copies, y_copies = {}, {}, {}

    def gather(chunk):
        blocks = pl.ds(chunk * group, group)
        for number in range(chunk * group, (chunk + 1) * group):
            if number > 0:
                z_copies[mirror(number)].wait_recv()
        for step, slot in ((2, 2), (1, 1), (-1, 3)):
            copy = send(
                arrived.at[0, blocks],
                arrived.at[slot, blocks],
                x_send.at[chunk, slot],
                x_recv.at[chunk, slot],
                at_x(step),
            )
            copy.start()
            x_copies[chunk, slot] = copy

    def share_weight(number):
        part = parts[number]
        for slot, needed in ((0, (0,)), (2, (1,)), (1, (4,))):
            for lane in needed:
                w_copies[number, lane].wait_recv()
            copy = send(
                weight.at[slot, part, half_rows],
                weight.at[slot, part, half_rows],
                f_send.at[number, slot],
                f_recv.at[number, slot],
                sibling,
            )
            copy.start()
            f_copies[number, slot] = copy

    gathered, shared = set(), set()

    def product(chunk, number):
        if chunk not in gathered:
            gathered.add(chunk)
            for slot in range(1, ring_x):
                x_copies[chunk, slot].wait_recv()
        if number not in shared:
            shared.add(number)
            for slot in range(ring_x - 1):
                f_copies[number, slot].wait_recv()
        blocks = pl.ds(chunk * group, group)
        left = jnp.concatenate(
            [arrived[slot, blocks].reshape(rows, features) for slot in range(ring_x)], axis=1
        )
        right = []
        first, end = bounds[number], bounds[number + 1]
        for index in range(first, end):
            right.append(
                jnp.concatenate(
                    [staged[index, x]] + [weight[slot, index] for slot in range(ring_x - 1)],
                    axis=1,
                )
            )
        product = lax.dot_general(
            left,
            jnp.concatenate(right, axis=0),
            (((1,), (1,)), ((), ())),
            preferred_element_type=jnp.float32,
        )
        for index in range(first, end):
            offset = (index - first) * units
            prod[chunk, index] = product[:, offset : offset + units]

    def message(chunk, lane, slot):
        sign = (1, -1)[lane]
        long = chunk // 2 == lane
        distance = 4 - slot
        takes = (slot - 1,) if slot > (0 if long else 1) else ()
        total = prod[chunk, distances.index(4 if distance == 4 else sign * distance)]
        for taken in takes:
            y_copies[lane, chunk, taken].wait_recv()
            total = total + part_in[lane, chunk, taken].astype(jnp.float32)
        part_out[lane, chunk, slot] = total.astype(jnp.bfloat16)
        copy = send(
            part_out.at[lane, chunk, slot],
            part_in.at[lane, chunk, slot],
            y_send.at[lane, chunk, slot],
            y_recv.at[lane, chunk, slot],
            at_y(sign),
        )
        copy.start()
        y_copies[lane, chunk, slot] = copy

    def start_reduce(chunk):
        long = chunk // 2
        message(chunk, long, 0)
        message(chunk, 1 - long, 1)

    def long_step(chunk):
        message(chunk, chunk // 2, 1)

    def both_step(chunk, slot):
        message(chunk, 0, slot)
        message(chunk, 1, slot)

    def finish(chunk):
        last = 3
        y_copies[0, chunk, last].wait_recv()
        y_copies[1, chunk, last].wait_recv()
        total = (
            prod[chunk, ring_y - 1]
            + part_in[0, chunk, last].astype(jnp.float32)
            + part_in[1, chunk, last].astype(jnp.float32)
        ).astype(jnp.bfloat16)
        for index in range(group):
            source = peer(chunk * group + index)
            gathered_grad[pl.ds(pl.multiple_of(source * cap, cap), cap), :] = total[
                index * cap : (index + 1) * cap
            ]

    piece_units = local.shape[0] // PIECES

    def weight_piece(piece):
        if piece == 0:
            for copy in saved_copies:
                copy.wait()
            flipped[...] = arrived[0].reshape(ring_e * cap, features).T
        base = (1 - core) * half_units if piece < PIECES // 2 else core * half_units
        start = base + (piece % (PIECES // 2)) * piece_units
        start = pl.multiple_of(start, piece_units)
        block = jnp.dot(
            flipped[...],
            saved[:, pl.ds(start, piece_units)],
            preferred_element_type=jnp.float32,
        )
        local[pl.ds(start, piece_units), :] = block.T.astype(jnp.bfloat16)

    theirs = pl.ds(pl.multiple_of((1 - core) * half_units, half_units), half_units)
    ours = pl.ds(pl.multiple_of(core * half_units, half_units), half_units)
    swap = send(local.at[theirs], other, g_send, g_recv, sibling)

    def advance(pieces):
        piece = next(pieces, None)
        if piece is not None:
            weight_piece(piece)
            if piece == PIECES // 2 - 1:
                swap.start()

    pieces = iter(range(PIECES))
    ops = {
        "g": gather,
        "W": send_weight,
        "s": share_weight,
        "p": product,
        "S": start_reduce,
        "L": long_step,
        "B": both_step,
        "f": finish,
        "a": lambda: advance(pieces),
    }
    for op in SCHEDULE:
        ops[op[0]](*[int(digit) for digit in op[1:]])

    swap.wait_recv()
    wg_ref[...] = (local[ours].astype(jnp.float32) + other[...].astype(jnp.float32)).astype(
        jnp.bfloat16
    )
    out = pltpu.make_async_copy(wg_ref, wg_hbm, out_sem.at[1])
    out.start()
    for chunk in range(CHUNKS):
        finish(chunk)
    hg_ref[...] = gathered_grad[...].T
    last_out = pltpu.make_async_copy(hg_ref, hg_hbm, out_sem.at[0])
    last_out.start()
    out.wait()
    last_out.wait()

    for copies in (w_copies, z_copies, x_copies, f_copies, y_copies):
        for copy in copies.values():
            copy.wait_send()
    swap.wait_send()


def hand_over(first_in, second_in, first_out, second_out, first, second, sem):
    pairs = ((first_in, first, first_out), (second_in, second, second_out))
    reads = [
        pltpu.make_async_copy(src, here, sem.at[0, index])
        for index, (src, here, _) in enumerate(pairs)
    ]
    writes = [
        pltpu.make_async_copy(here, dst, sem.at[1, index])
        for index, (_, here, dst) in enumerate(pairs)
    ]
    for read in reads:
        read.start()
    for read, write in zip(reads, writes):
        read.wait()
        write.start()
    for write in writes:
        write.wait()


def per_device(grad_out, gates, routes, hidden, w_down):
    ring_e = lax.axis_size("expert")
    ring_t = lax.axis_size("tensor")
    ring_x = RING_X
    ring_y = ring_t // ring_x
    tokens, features = grad_out.shape
    slots, units = hidden.shape[2], hidden.shape[3]
    cap = slots // ring_e
    own_units = units // ring_t
    rows = slots // CHUNKS
    half_y = ring_y // 2
    sublanes = -(-ring_e // 16) * 16
    bf16, f32 = jnp.bfloat16, jnp.float32
    dma = pltpu.SemaphoreType.DMA
    hbm = pl.BlockSpec(memory_space=pl.ANY)
    hidden_grad, weight_grad = pl.pallas_call(
        functools.partial(kernel, ring_e, ring_x, ring_y),
        out_shape=(
            jax.ShapeDtypeStruct((own_units, slots), bf16),
            jax.ShapeDtypeStruct((units // 2, features), bf16),
        ),
        in_specs=[hbm] * 5,
        out_specs=(hbm, hbm),
        scratch_shapes=[
            pltpu.VMEM((tokens, features), bf16),
            pltpu.VMEM((2, tokens), f32),
            pltpu.VMEM((2, tokens), jnp.int32),
            pltpu.VMEM((slots, units), bf16),
            pltpu.VMEM((ring_y, ring_x, own_units, features), bf16),
            pltpu.VMEM((ring_x - 1, ring_y, own_units, features), bf16),
            pltpu.VMEM((ring_x, ring_e, cap, features), bf16),
            pltpu.VMEM((ring_e, cap, features), bf16),
            pltpu.VMEM((sublanes, tokens), jnp.int32),
            pltpu.VMEM((sublanes, tokens), f32),
            pltpu.VMEM((features, slots), bf16),
            pltpu.VMEM((CHUNKS, ring_y, rows, own_units), f32),
            pltpu.VMEM((2, CHUNKS, half_y, rows, own_units), bf16),
            pltpu.VMEM((2, CHUNKS, half_y, rows, own_units), bf16),
            pltpu.VMEM((units, features), bf16),
            pltpu.VMEM((units // 2, features), bf16),
            pltpu.VMEM((slots, own_units), bf16),
            pltpu.VMEM((own_units, slots), bf16),
            pltpu.VMEM((units // 2, features), bf16),
            dma((3,)),
            dma((ring_e,)),
            dma((ring_y,)),
            dma((ring_e,)),
            dma((ring_e,)),
            dma((half_y, 6)),
            dma((half_y, 6)),
            dma((half_y, ring_x - 1)),
            dma((half_y, ring_x - 1)),
            dma((CHUNKS, ring_x)),
            dma((CHUNKS, ring_x)),
            dma((2, CHUNKS, half_y)),
            dma((2, CHUNKS, half_y)),
            dma,
            dma,
            dma((2,)),
        ],
        compiler_params=pltpu.CompilerParams(
            collective_id=0, has_side_effects=True, vmem_limit_bytes=60 * 1024 * 1024
        ),
        cost_estimate=pl.CostEstimate(
            flops=4 * units * slots * features,
            bytes_accessed=2 * units * (slots + 2 * features),
            transcendentals=0,
        ),
    )(
        grad_out,
        gates.T,
        routes.T,
        hidden.reshape(ring_e, cap, units),
        w_down.reshape(ring_y, ring_x, own_units, features),
    )
    hidden_grad, weight_grad = pl.pallas_call(
        hand_over,
        out_shape=(
            jax.ShapeDtypeStruct(hidden_grad.shape, bf16),
            jax.ShapeDtypeStruct(weight_grad.shape, bf16),
        ),
        in_specs=[hbm] * 2,
        out_specs=(hbm, hbm),
        scratch_shapes=[
            pltpu.VMEM(hidden_grad.shape, bf16),
            pltpu.VMEM(weight_grad.shape, bf16),
            dma((2, 2)),
        ],
        compiler_params=pltpu.CompilerParams(vmem_limit_bytes=60 * 1024 * 1024),
    )(hidden_grad, weight_grad)
    return hidden_grad[None, None], weight_grad[None]


def solution(mesh):
    placed = (
        P(("dp", "expert"), "tensor"),
        P(("dp", "expert"), None),
        P(("dp", "expert"), None),
        P("dp", "expert", None, None),
        P("expert", None, "tensor"),
    )
    return jax.shard_map(
        per_device,
        mesh=mesh,
        in_specs=placed,
        out_specs=(P("dp", "expert", "tensor", None), P("expert", "dp", "tensor")),
        check_vma=False,
    )
```

time: 62.6 us -> 53.7 us (0.86)
  the two profiles are of different devices: /device:TPU:4 before, /device:TPU:8 now
where the time goes in v2:
time: 53.7 us; the launch traced here: 53.5 us
  Pallas kernels  52.9 us (99%)
  between operations  0.64 us (1%)
    pallas_call x1, Pallas kernels, per_device(): pl.pallas_call(functools.partial(kernel, ring_e, ring_x, ring_y), out_sha...  50.9 us
    pallas_call x1, Pallas kernels, per_device(): pl.pallas_call(hand_over, out_shape=(jax.ShapeDtypeStruct(hidden_grad.sha...  1.98 us

profile of v2, /device:TPU:8, one launch (start us, length us, event | category | flops | bytes accessed | tf_op | source)
XLA Modules:
  0.0 53.5 jit_solution(950078429892905552)
XLA Ops:
  0.6 50.9 %shard_map.68 = (bf16[128,768]{1,0:T(8,128)(2,1)}, bf16[2048,128]{1,0:T(8,128)(2,1)}) custom-call(bf16[256,128]{1,0:T(8,128)(2,1)} %grad_hbm.1, f32[2,256]{1,0:T(2,128)} %bitcast.8, s32[2,256]{1,0:T(2,128)} %bitcast.9, bf16[12,64,4096]{2,1,0:T(8,128)(2,1)} %bitcast.6, bf16[8,4,128,128]{3,2,1,0:T(8,128)(2,1)} %bitcast.7), custom_call_target="tpu_custom_call" | custom-call | flops 1610612736 | bytes 8388608 | tf_op jit(solution)/shard_map/pallas_call | solution.py:453
  51.6 2.0 %shard_map.69 = (bf16[128,768]{1,0:T(8,128)(2,1)}, bf16[2048,128]{1,0:T(8,128)(2,1)}) custom-call(bf16[128,768]{1,0:T(8,128)(2,1)} %get-tuple-element.6.first_in, bf16[2048,128]{1,0:T(8,128)(2,1)} %get-tuple-element.7.second_in), custom_call_target="tpu_custom_call" | custom-call | tf_op jit(solution)/shard_map/pallas_call | solution.py:513

commit v3 on v2

--- a/solution.py
+++ b/solution.py
@@ -15,7 +15,7 @@
 SCHEDULE = tuple(
     step
     for steps in (
-        ("W0", "W1", "W2", "g0", "g1", "g2", "g3", "s0", "s1"),
+        ("g0", "g1", "g2", "g3", "s0", "s1"),
         ("s2", "a", "a", "p00", "S0", "p10", "S1", "p20", "S2"),
         ("p30", "S3", "a", "L0", "a", "L1", "a", "L2", "a"),
         ("L3", "p01", "B02", "a", "p11", "B12", "a", "p21", "B22"),
@@ -205,13 +205,10 @@
             z_recv.at[mirror(number)],
             {"expert": peer(number)},
         )
-        copy.start()
         z_copies[number] = copy
 
     half_rows = pl.ds(pl.multiple_of(core * (units // 2), units // 2), units // 2)
     w_copies = {}
-    for copy in staged_copies:
-        copy.wait()
 
     def chip(step):
         return lax.rem(x + step + ring_x, ring_x)
@@ -226,8 +223,30 @@
                 w_recv.at[number, lane],
                 at_x(step),
             )
+            w_copies[number, lane] = copy
+
+    for number in range(len(parts)):
+        send_weight(number)
+
+    def start_dispatch():
+        for copy in z_copies.values():
             copy.start()
-            w_copies[number, lane] = copy
+
+    def start_weight():
+        for copy in staged_copies:
+            copy.wait()
+        for copy in w_copies.values():
+            copy.start()
+
+    @pl.when(core == 0)
+    def _():
+        start_dispatch()
+        start_weight()
+
+    @pl.when(core == 1)
+    def _():
+        start_weight()
+        start_dispatch()
 
     saved_copies = []
     for number in range(ring_e):
@@ -384,7 +403,6 @@
     pieces = iter(range(PIECES))
     ops = {
         "g": gather,
-        "W": send_weight,
         "s": share_weight,
         "p": product,
         "S": start_reduce,

time: 53.7 us -> 54.1 us (level)
  no operation moved by 1% of the time
where the time goes in v3:
time: 54.1 us; the launch traced here: 53.9 us
  Pallas kernels  53.3 us (99%)
  between operations  0.64 us (1%)
    pallas_call x1, Pallas kernels, per_device(): pl.pallas_call(functools.partial(kernel, ring_e, ring_x, ring_y), out_sha...  51.3 us
    pallas_call x1, Pallas kernels, per_device(): pl.pallas_call(hand_over, out_shape=(jax.ShapeDtypeStruct(hidden_grad.sha...  1.98 us

profile of v3, /device:TPU:8, one launch (start us, length us, event | category | flops | bytes accessed | tf_op | source)
XLA Modules:
  0.0 53.9 jit_solution(1951499844299946218)
XLA Ops:
  0.6 51.3 %shard_map.68 = (bf16[128,768]{1,0:T(8,128)(2,1)}, bf16[2048,128]{1,0:T(8,128)(2,1)}) custom-call(bf16[256,128]{1,0:T(8,128)(2,1)} %grad_hbm.1, f32[2,256]{1,0:T(2,128)} %bitcast.8, s32[2,256]{1,0:T(2,128)} %bitcast.9, bf16[12,64,4096]{2,1,0:T(8,128)(2,1)} %bitcast.6, bf16[8,4,128,128]{3,2,1,0:T(8,128)(2,1)} %bitcast.7), custom_call_target="tpu_custom_call" | custom-call | flops 1610612736 | bytes 8388608 | tf_op jit(solution)/shard_map/pallas_call | solution.py:471
  51.9 2.0 %shard_map.69 = (bf16[128,768]{1,0:T(8,128)(2,1)}, bf16[2048,128]{1,0:T(8,128)(2,1)}) custom-call(bf16[128,768]{1,0:T(8,128)(2,1)} %get-tuple-element.6.first_in, bf16[2048,128]{1,0:T(8,128)(2,1)} %get-tuple-element.7.second_in), custom_call_target="tpu_custom_call" | custom-call | tf_op jit(solution)/shard_map/pallas_call | solution.py:531
